TPU v7x, 32 devices: a whole 2x2x4 slice. The times are simulated.
32 devices in a mesh: gx: 4 (over y, x), gz: 8 (over z, core).
Axes of the slice: x: 2, y: 2, z: 4, core: 2. Of those that a mesh axis runs over, the one named last changes fastest.
Arguments:
- adjoint: float32 [3, 128, 64, 512], P(None, 'gz', 'gx')
- base_flow: float32 [2, 128, 64, 512], P(None, 'gz', 'gx'), may hold values from 0.5 to 1.5
- conductance: float32 [128, 64, 512], P('gz', 'gx'), may hold values from 20 to 80
- ground_mask: int32 [64, 512], P('gx'), may hold values 0 or 1
- turbine_cells: int32 [3, 100], replicated, may hold values from 0 to 511, as said below
- yaw_bin: int32 [100], replicated, may hold values from 0 to 11
- yaw_table: float32 [3, 12], replicated, may hold values from -20 to 20
Outputs:
- adjoint_out: float32 [3, 128, 64, 512], P(None, 'gz', 'gx')
Inputs may be any that keep to these rules, and one draw needn't show every extreme that they name: `turbine_cells`: row 0 holds a turbine's vertical cell, below 128; row 1 its streamwise cell, below 64; row 2 its spanwise cell, below 512. Turbines may share a cell. Some turbine stands in the cell (0, 0, 0) and some in the cell (127, 63, 511).
All inputs are finite; a program needn't handle non-finite values. No bound on the sum of `ground_mask` on one device may be relied on, other than what follows from the above.
Results may differ from a plain program's by a relative error of at most 0.0003.
Values sent between devices are 32-bit elements; how exact they have to be, the bound alone decides.
No kernel may reach another device: no remote copies, remote signals or barrier semaphores. Data moves between devices by JAX's collectives and lax.ppermute only.
A program may use at most 192 MiB of HBM per device.

v0:
```python
import jax
import jax.numpy as jnp
from jax import lax
from jax.sharding import PartitionSpec as P

SWEEPS = 2
PSEUDO_STEP = 0.2
LATERAL_VISC = 1.0


def padded_2(cells, sides, width):
    for axis, dim in sides:
        count = lax.axis_size(axis)
        ends = count - 1
        head = lax.slice_in_dim(cells, 0, width, axis=dim)
        tail = lax.slice_in_dim(cells, cells.shape[dim] - width, cells.shape[dim], axis=dim)
        cells = jnp.concatenate(
            [
                lax.ppermute(tail, axis, [(i, (i + 1) % count) for i in range(ends)]),
                cells,
                lax.ppermute(head, axis, [((i + 1) % count, i) for i in range(ends)]),
            ],
            axis=dim,
        )
    return cells


def thomas(sub_diag, main_diag, super_diag, right_side):

    def forward(carry, row_values):
        ratio_prev, value_prev = carry
        lower_c, centre, upper_c, target = row_values
        pivot = centre - lower_c * ratio_prev
        ratio_next = upper_c / pivot
        value_next = (target - lower_c * value_prev) / pivot
        return ((ratio_next, value_next), (ratio_next, value_next))

    start = (
        jnp.zeros(super_diag.shape[1:], jnp.float32),
        jnp.zeros(right_side.shape[1:], jnp.float32),
    )
    _, (ratios, values) = lax.scan(forward, start, (sub_diag, main_diag, super_diag, right_side))

    def backward(later, row_values):
        ratio_here, value_here = row_values
        result = value_here - ratio_here * later
        return (result, result)

    _, solved = lax.scan(
        backward, jnp.zeros(right_side.shape[1:], jnp.float32), (ratios, values), reverse=True
    )
    return solved


def lateral(adjoint_now, base_flow, x_minus, x_plus):
    padded_y = jnp.pad(adjoint_now, ((0, 0), (0, 0), (0, 0), (1, 1)))
    y_minus = padded_y[:, :, :, :-2]
    y_plus = padded_y[:, :, :, 2:]
    advect = base_flow[0:1] * (x_plus - x_minus) * 0.5 + base_flow[1:2] * (y_plus - y_minus) * 0.5
    spread = x_plus + x_minus + y_plus + y_minus - 4.0 * adjoint_now
    return adjoint_now + PSEUDO_STEP * (advect + LATERAL_VISC * spread)


def per_device(adjoint, base_flow, conductance, ground_mask, turbine_cells, yaw_bin, yaw_table):
    z_cells = adjoint.shape[1]
    x_cells = adjoint.shape[2]
    y_cells = adjoint.shape[3]
    columns = x_cells * y_cells
    slab_index = lax.axis_index("gz")
    strip_index = lax.axis_index("gx")
    bin_count = yaw_table.shape[1]
    selector = (yaw_bin[None, :] == jnp.arange(bin_count, dtype=jnp.int32)[:, None]).astype(
        jnp.float32
    )
    strengths = jnp.dot(yaw_table, selector, precision=lax.Precision.HIGHEST)
    local_z = turbine_cells[0] - slab_index * z_cells
    local_x = turbine_cells[1] - strip_index * x_cells
    inside = (local_z >= 0) & (local_z < z_cells) & (local_x >= 0) & (local_x < x_cells)
    weights = strengths * inside.astype(jnp.float32)[None, :]
    source = (
        jnp.zeros(adjoint.shape, jnp.float32)
        .at[
            :,
            jnp.clip(local_z, 0, z_cells - 1),
            jnp.clip(local_x, 0, x_cells - 1),
            turbine_cells[2],
        ]
        .add(weights)
    )
    cond_cols = conductance.reshape(z_cells, columns)
    wall_flag = ground_mask.reshape(columns).astype(jnp.float32)
    bottom_face = jnp.where(slab_index == 0, cond_cols[0] * wall_flag, cond_cols[0])
    low_face = jnp.concatenate([bottom_face[None], cond_cols[1:]], 0)
    zero_row = jnp.zeros((1, columns), jnp.float32)
    current = adjoint
    interior = z_cells - 1
    first_link = jnp.where(slab_index == 0, jnp.zeros((columns,), jnp.float32), cond_cols[0])
    sub_inner = jnp.concatenate([zero_row, -cond_cols[1:interior]], 0)
    super_inner = -cond_cols[1:z_cells]
    main_inner = 1.0 + low_face[:interior] + cond_cols[1:z_cells]
    spike_right = jnp.zeros((interior, 2, columns), jnp.float32)
    spike_right = spike_right.at[0, 0].set(first_link)
    spike_right = spike_right.at[interior - 1, 1].set(cond_cols[z_cells - 1])
    spikes = thomas(sub_inner[:, None], main_inner[:, None], super_inner[:, None], spike_right)
    spike_below = spikes[:, 0]
    spike_above = spikes[:, 1]
    face_part = jnp.stack(
        [
            cond_cols[0],
            spike_below[0],
            spike_above[0],
            spike_below[interior - 1],
            spike_above[interior - 1],
            cond_cols[z_cells - 1],
        ],
        0,
    )[None]
    face_all = lax.all_gather(face_part, "gz", axis=0, tiled=True)
    next_faces = jnp.concatenate([face_all[1:], jnp.zeros_like(face_all[:1])], 0)
    lower_link = -face_all[:, 5]
    upper_link = -next_faces[:, 0]
    centre = 1.0 + face_all[:, 5] + next_faces[:, 0]
    red_sub = lower_link * face_all[:, 3]
    red_main = lower_link * face_all[:, 4] + centre + upper_link * next_faces[:, 1]
    red_super = upper_link * next_faces[:, 2]
    for sweep_index in range(SWEEPS):
        padded = padded_2(current, (("gx", 2),), 1)
        right_side = lateral(current, base_flow, padded[:, :, :-2], padded[:, :, 2:]) + source
        stacked = jnp.moveaxis(right_side.reshape(3, z_cells, columns), 1, 0)
        local_part = thomas(
            sub_inner[:, None], main_inner[:, None], super_inner[:, None], stacked[:interior]
        )
        right_part = jnp.concatenate(
            [local_part[0], local_part[interior - 1], stacked[z_cells - 1]], 0
        )[None]
        right_all = lax.all_gather(right_part, "gz", axis=0, tiled=True)
        next_first = jnp.concatenate([right_all[1:, 0:3], jnp.zeros_like(right_all[:1, 0:3])], 0)
        red_right = (
            right_all[:, 6:9]
            - lower_link[:, None] * right_all[:, 3:6]
            - upper_link[:, None] * next_first
        )
        interface = thomas(red_sub[:, None], red_main[:, None], red_super[:, None], red_right)
        prev_top = lax.dynamic_index_in_dim(
            interface, jnp.maximum(slab_index - 1, 0), 0, keepdims=False
        )
        prev_top = prev_top * (slab_index > 0).astype(jnp.float32)
        own_top = lax.dynamic_index_in_dim(interface, slab_index, 0, keepdims=False)
        inner_values = (
            local_part
            + spike_below[:, None] * prev_top[None]
            + spike_above[:, None] * own_top[None]
        )
        solved = jnp.concatenate([inner_values, own_top[None]], 0)
        current = jnp.moveaxis(solved, 0, 1).reshape(adjoint.shape)
    return current


def solution(mesh):
    in_specs = (
        P(None, "gz", "gx", None),
        P(None, "gz", "gx", None),
        P("gz", "gx", None),
        P("gx", None),
        P(),
        P(),
        P(),
    )
    out_specs = P(None, "gz", "gx", None)
    return jax.shard_map(
        per_device, mesh=mesh, in_specs=in_specs, out_specs=out_specs, check_vma=False
    )
```

profile of v0, /device:TPU:0, one launch (start us, length us, event | category | flops | bytes accessed | tf_op | source)
XLA Modules:
  0.0 549.8 jit_solution(8781116341680570288)
XLA Ops:
  10.7 6.1 %collective-permute-start.1 = (f32[3,16,1,512]{3,1,2,0:T(8,128)}, f32[3,16,1,512]{3,1,2,0:T(8,128)}, u32[]{:S(2)}, u32[]{:S(2)}) collective-permute-start(f32[3,16,1,512]{3,1,2,0:T(8,128)} %copy.89), channel_id=1, source_target_pairs={{0,8},{8,16},{16,24},{1,9},{9,17},{17,25},{2,10},{10,18},{18,26},{... | collective-permute-start | bytes 294920 | tf_op jit(solution)/shard_map/ppermute | solution.py:19
  23.8 12.7 %while.174 = (s32[]{:T(128)}, f32[1,8192]{1,0:T(1,128)S(1)}, f32[2,8192]{1,0:T(2,128)S(1)}, f32[15,1,8192]{2,1,0:T(1,128)}, f32[15,2,8192]{2,1,0:T(2,128)S(1)}, ...) while((s32[]{:T(128)}, f32[1,8192]{1,0:T(1,128)S(1)}, ...), condition=%wide.region_6.7_spmd.clone, body=%wide.region_5.6_spmd.clone.sunk | while | flops 98307 | bytes 590460 | solution.py:42
  37.9 33.9 %while.175 = (s32[]{:T(128)}, f32[2,8192]{1,0:T(2,128)}, f32[15,2,8192]{2,1,0:T(2,128)S(1)}, f32[15,2,8192]{2,1,0:T(2,128)S(1)}, f32[15,1,8192]{2,1,0:T(1,128)}, /*index=5*/s32[]{:T(128)}, s32[]{:T(128)}, s32[]{:T(128)}) while((s32[]{:T(128)}, f32[2,8192]{1,0:T(2,128)}, f32[15,2,8192]{2,1,0:T(2,128)S(1)}, ...), condition=%wide.region_8.9_spmd.clone, body=%wide.region_7.8_spmd.clone.sunk | while | flops 49156 | bytes 360563 | solution.py:49
  76.9 21.5 %broadcast_in_dim.134 = f32[3,16,16,512]{0,3,2,1:T(8,128)} broadcast(f32[]{:T(128)} %constant.348.clone.1), dimensions={} | broadcast | bytes 1572868 | tf_op jit(solution)/shard_map/broadcast_in_dim | solution.py:81
  98.3 12.3 %scatter_fusion = f32[3,16,16,512]{0,3,2,1:T(8,128)} fusion(f32[3,16,16,512]{0,3,2,1:T(8,128)} %broadcast_in_dim.134, s32[100]{0:T(128)S(1)} %fusion.30, f32[100,3]{1,0:T(8,128)S(1)} %copy.71), kind=kCustom, calls=%fused_computation | custom fusion | flops 300 | bytes 4800 | tf_op jit(solution)/shard_map/scatter-add | solution.py:88
  110.6 38.3 %copy.72 = f32[3,16,16,512]{3,2,1,0:T(8,128)S(1)} copy(f32[3,16,16,512]{0,3,2,1:T(8,128)} %scatter_fusion) | data formatting | bytes 3145728 | tf_op jit(solution)/shard_map/scatter-add | solution.py:88
  151.0 6.9 %add_add_fusion.1 = f32[3,16,16,512]{3,2,1,0:T(8,128)} fusion(f32[3,16,16,512]{3,2,1,0:T(8,128)S(1)} %copy.72, f32[3,16,16,512]{3,2,1,0:T(8,128)} %param.31, f32[3,16,1,512]{3,2,1,0:T(1,128)S(1)} %copy.68, f32[3,16,1,512]{3,2,1,0:T(1,128)S(1)} %copy.70, f32[16,16,512]{2,1,0:T(8,128)S(1)} %get-tuple-element.1237, f32[16,16,512]{2,1,0:T(8,128)S(1)} %get-tuple-element.1236), kind=kLoop, calls=%fused_computation.89 | loop fusion | flops 6684672 | bytes 5963776 | tf_op jit(solution)/shard_map/add | solution.py:128
  164.0 49.0 %while.172 = (s32[]{:T(128)}, f32[1,8192]{1,0:T(1,128)}, f32[3,8192]{1,0:T(4,128)}, f32[15,1,8192]{2,1,0:T(1,128)}, f32[15,3,8192]{2,1,0:T(4,128)S(1)}, /*index=...) while((s32[]{:T(128)}, f32[1,8192]{1,0:T(1,128)}, ...), condition=%wide.region_2.3_spmd.clone, body=%wide.region_1.2_spmd.clone.sunk | while | flops 131075 | bytes 754300 | solution.py:42
  214.7 46.1 %while.173 = (s32[]{:T(128)}, f32[3,8192]{1,0:T(4,128)}, f32[15,3,8192]{2,1,0:T(4,128)S(1)}, f32[15,3,8192]{2,1,0:T(4,128)}, f32[15,1,8192]{2,1,0:T(1,128)}, /*index=5*/s32[]{:T(128)}, s32[]{:T(128)}, s32[]{:T(128)}) while((s32[]{:T(128)}, f32[3,8192]{1,0:T(4,128)}, f32[15,3,8192]{2,1,0:T(4,128)S(1)}, f32[15,3,8192]{2,1,0:T(4,128)}, ...), condition=%wide.region_4.5_spmd.clone, body=%wide.region_3.4_spmd.clone.sunk | while | flops 73732 | bytes 524403 | solution.py:49
  263.1 2.7 copy_bitcast_fusion.2
  267.3 5.1 slice_negate_fusion.1
  273.5 37.6 %all-gather.12.cloned.1.call-done = f32[8,9,8192]{2,1,0:T(8,128)} async-done(((f32[1,9,8192]{2,1,0:T(8,128)}), f32[8,9,8192]{2,1,0:T(8,128)}) %all-gather.12.cloned.1.call-update) | async-done | bytes 2359312 | tf_op jit(solution)/shard_map/all_gather | solution.py:136
  312.9 4.6 fusion.18
  319.5 26.3 %while.176 = (s32[]{:T(128)}, f32[1,8192]{1,0:T(1,128)}, f32[3,8192]{1,0:T(4,128)}, f32[8,1,8192]{2,1,0:T(1,128)}, f32[8,3,8192]{2,1,0:T(4,128)}, /*index=5*/f32...) while((s32[]{:T(128)}, f32[1,8192]{1,0:T(1,128)}, ...), condition=%wide.region_10.11_spmd.clone, body=%wide.region_9.10_spmd.clone.sunk | while | flops 131075 | bytes 853112 | solution.py:42
  346.9 25.1 %while.177 = (s32[]{:T(128)}, f32[3,8192]{1,0:T(4,128)}, f32[8,3,8192]{2,1,0:T(4,128)}, f32[8,3,8192]{2,1,0:T(4,128)}, f32[8,1,8192]{2,1,0:T(1,128)}, /*index=5*/s32[]{:T(128)}, s32[]{:T(128)}, s32[]{:T(128)}) while((s32[]{:T(128)}, f32[3,8192]{1,0:T(4,128)}, f32[8,3,8192]{2,1,0:T(4,128)}, f32[8,3,8192]{2,1,0:T(4,128)}, ...), condition=%wide.region_12.13_spmd.clone, body=%wide.region_11.12_spmd.clone.sunk | while | flops 73732 | bytes 622707 | solution.py:49
  376.9 2.9 reshape.259
  382.0 5.2 collective-permute-start.3
  395.2 29.7 %while.178 = (s32[]{:T(128)}, f32[1,8192]{1,0:T(1,128)S(1)}, f32[3,8192]{1,0:T(4,128)S(1)}, f32[15,1,8192]{2,1,0:T(1,128)S(1)}, f32[15,3,8192]{2,1,0:T(4,128)S(1...) while((s32[]{:T(128)}, f32[1,8192]{1,0:T(1,128)S(1)}, ...), condition=%wide.region_14.15_spmd.clone, body=%wide.region_13.14_spmd.clone.sunk | while | flops 131075 | bytes 819328 | solution.py:42
  426.5 16.7 %while.179 = (s32[]{:T(128)}, f32[3,8192]{1,0:T(4,128)S(1)}, f32[15,3,8192]{2,1,0:T(4,128)S(1)}, f32[15,3,8192]{2,1,0:T(4,128)}, f32[15,1,8192]{2,1,0:T(1,128)S(1)}, /*index=5*/s32[]{:T(128)}, s32[]{:T(128)}, s32[]{:T(128)}) while((s32[]{:T(128)}, f32[3,8192]{1,0:T(4,128)S(1)}, f32[15,3,8192]{2,1,0:T(4,128)S(1)}, ...), condition=%wide.region_16.17_spmd.clone, body=%wide.region_15.16_spmd.clone.sunk | while | flops 73732 | bytes 589939 | solution.py:49
  444.3 47.8 %all-gather.14.cloned.1.call-done = f32[8,9,8192]{2,1,0:T(8,128)} async-done(((f32[1,9,8192]{2,1,0:T(8,128)}), f32[8,9,8192]{2,1,0:T(8,128)}) %all-gather.14.cloned.1.call-update) | async-done | bytes 2359312 | tf_op jit(solution)/shard_map/all_gather | solution.py:136
  493.8 4.9 fusion.16
  500.1 21.0 %while.180 = (s32[]{:T(128)}, f32[1,8192]{1,0:T(1,128)S(1)}, f32[3,8192]{1,0:T(4,128)S(1)}, f32[8,1,8192]{2,1,0:T(1,128)S(1)}, f32[8,3,8192]{2,1,0:T(4,128)}, /*...) while((s32[]{:T(128)}, f32[1,8192]{1,0:T(1,128)S(1)}, ...), condition=%wide.region_18.19_spmd.clone, body=%wide.region_17.18_spmd.clone.sunk | while | flops 131075 | bytes 787068 | solution.py:42
  522.2 14.0 %while.181 = (s32[]{:T(128)}, f32[3,8192]{1,0:T(4,128)S(1)}, f32[8,3,8192]{2,1,0:T(4,128)}, f32[8,3,8192]{2,1,0:T(4,128)}, f32[8,1,8192]{2,1,0:T(1,128)S(1)}, /*index=5*/s32[]{:T(128)}, s32[]{:T(128)}, s32[]{:T(128)}) while((s32[]{:T(128)}, f32[3,8192]{1,0:T(4,128)S(1)}, f32[8,3,8192]{2,1,0:T(4,128)}, f32[8,3,8192]{2,1,0:T(4,128)}, ...), condition=%wide.region_20.21_spmd.clone, body=%wide.region_19.20_spmd.clone.sunk | while | flops 73732 | bytes 557171 | solution.py:49
  540.5 2.8 copy.83
  (401 shorter events, 336.4 us)
Async XLA Ops:
  6.5 70.0 %copy-start = (f32[3,12]{1,0:T(4,128)S(1)}, f32[3,12]{1,0:T(4,128)}, u32[]{:S(2)}) copy-start(f32[3,12]{1,0:T(4,128)} %param.37) | copy-start | bytes 436
  6.5 11.5 %copy-start.15 = (f32[16,16,512]{2,1,0:T(8,128)S(1)}, f32[16,16,512]{2,1,0:T(8,128)}, u32[]{:S(2)}) copy-start(f32[16,16,512]{2,1,0:T(8,128)} %param.33) | copy-start | bytes 1572868
  6.5 12.2 %copy-start.22 = (s32[16,512]{1,0:T(8,128)S(1)}, s32[16,512]{1,0:T(8,128)}, u32[]{:S(2)}) copy-start(s32[16,512]{1,0:T(8,128)} %param.34) | copy-start | bytes 98308
  6.5 259.3 %all-gather.10.cloned.1.call-start = ((), (), s32[]{:S(2)}) async-start(), calls=%async_computation | async-start | bytes 2359296 | tf_op jit(solution)/shard_map/all_gather | solution.py:118
  8.8 140.2 %collective-permute-start = (f32[3,16,1,512]{3,1,2,0:T(8,128)}, f32[3,16,1,512]{3,1,2,0:T(8,128)}, u32[]{:S(2)}, u32[]{:S(2)}) collective-permute-start(f32[3,16,1,512]{3,1,2,0:T(8,128)} %copy.88), channel_id=1, source_target_pairs={{8,0},{16,8},{24,16},{9,1},{17,9},{25,17},{10,2},{18,10},{26,18},{... | collective-permute-start | bytes 294920 | tf_op jit(solution)/shard_map/ppermute | solution.py:21
  10.7 139.2 %collective-permute-start.1 = (f32[3,16,1,512]{3,1,2,0:T(8,128)}, f32[3,16,1,512]{3,1,2,0:T(8,128)}, u32[]{:S(2)}, u32[]{:S(2)}) collective-permute-start(f32[3,16,1,512]{3,1,2,0:T(8,128)} %copy.89), channel_id=1, source_target_pairs={{0,8},{8,16},{16,24},{1,9},{9,17},{17,25},{2,10},{10,18},{18,26},{... | collective-permute-start | bytes 294920 | tf_op jit(solution)/shard_map/ppermute | solution.py:19
  36.6 35.3 %copy-start.21 = (f32[1,1,16,512]{3,2,1,0:T(8,128)S(1)}, f32[1,1,16,512]{3,2,1,0:T(8,128)}, u32[]{:S(2)}) copy-start(f32[1,1,16,512]{3,2,1,0:T(8,128)} %get-tuple-element.1244) | copy-start | bytes 98308
  36.6 35.4 %copy-start.20 = (f32[1,1,16,512]{3,1,2,0:T(1,128)S(1)}, f32[1,1,16,512]{3,1,2,0:T(1,128)}, u32[]{:S(2)}) copy-start(f32[1,1,16,512]{3,1,2,0:T(1,128)} %copy-done.19) | copy-start | bytes 98308
  73.0 3.5 copy-start.23
  73.0 3.6 copy-start.24
  73.0 238.1 %all-gather.12.cloned.1.call-start = ((), (), s32[]{:S(2)}) async-start(), calls=%async_computation.1 | async-start | bytes 4718592 | tf_op jit(solution)/shard_map/all_gather | solution.py:136
  76.5 74.5 %copy-start.5 = (f32[16,16,512]{2,1,0:T(8,128)}, f32[16,16,512]{2,1,0:T(8,128)S(1)}, u32[]{:S(2)}) copy-start(f32[16,16,512]{2,1,0:T(8,128)S(1)} %get-tuple-element.1236) | copy-start | bytes 1572868
  76.5 74.5 %copy-start.7 = (f32[16,16,512]{2,1,0:T(8,128)}, f32[16,16,512]{2,1,0:T(8,128)S(1)}, u32[]{:S(2)}) copy-start(f32[16,16,512]{2,1,0:T(8,128)S(1)} %get-tuple-element.1237) | copy-start | bytes 1572868
  160.5 2.0 copy-start.2
  262.8 229.4 %all-gather.14.cloned.1.call-start = ((), (), s32[]{:S(2)}) async-start(), calls=%async_computation.2 | async-start | bytes 4718592 | tf_op jit(solution)/shard_map/all_gather | solution.py:136
  380.0 7.3 %collective-permute-start.2 = (f32[3,16,1,512]{3,1,2,0:T(8,128)S(1)}, f32[3,16,1,512]{3,1,2,0:T(8,128)}, u32[]{:S(2)}, u32[]{:S(2)}) collective-permute-start(f32[3,16,1,512]{3,1,2,0:T(8,128)S(1)} %copy.75), channel_id=1, source_target_pairs={{8,0},{16,8},{24,16},{9,1},{17,9},{25,17},{10,2},{18,10},{26,18},{... | collective-permute-start | bytes 294920 | tf_op jit(solution)/shard_map/ppermute | solution.py:21
  382.0 7.1 %collective-permute-start.3 = (f32[3,16,1,512]{3,1,2,0:T(8,128)}, f32[3,16,1,512]{3,1,2,0:T(8,128)}, u32[]{:S(2)}, u32[]{:S(2)}) collective-permute-start(f32[3,16,1,512]{3,1,2,0:T(8,128)} %copy.77), channel_id=1, source_target_pairs={{0,8},{8,16},{16,24},{1,9},{9,17},{17,25},{2,10},{10,18},{18,26},{... | collective-permute-start | bytes 294920 | tf_op jit(solution)/shard_map/ppermute | solution.py:19
  387.2 2.9 copy-start.6
  387.2 2.9 copy-start.8
  443.3 50.5 %copy-start.12 = (f32[8,8192]{1,0:T(8,128)S(1)}, f32[8,8192]{1,0:T(8,128)}, u32[]{:S(2)}) copy-start(f32[8,8192]{1,0:T(8,128)} %get-tuple-element.1250) | copy-start | bytes 786436
  443.3 50.5 %copy-start.14 = (f32[8,8192]{1,0:T(8,128)S(1)}, f32[8,8192]{1,0:T(8,128)}, u32[]{:S(2)}) copy-start(f32[8,8192]{1,0:T(8,128)} %get-tuple-element.1251) | copy-start | bytes 786436
  522.2 15.0 %copy-start.3 = (f32[15,8192]{1,0:T(8,128)S(1)}, f32[15,8192]{1,0:T(8,128)}, u32[]{:S(2)}) copy-start(f32[15,8192]{1,0:T(8,128)} %get-tuple-element.1253) | copy-start | bytes 1474564
  522.2 15.0 %copy-start.4 = (f32[15,8192]{1,0:T(8,128)S(1)}, f32[15,8192]{1,0:T(8,128)}, u32[]{:S(2)}) copy-start(f32[15,8192]{1,0:T(8,128)} %get-tuple-element.1254) | copy-start | bytes 1474564
  538.4 4.9 copy-start.1
  (9 other events, 11.1 us)
Sparse Core Ops, SparseCore 0:
  73.1 30.1 all-gather.9
  262.9 48.1 all-gather.11
  444.4 47.7 all-gather.13
where the time goes:
time: 559 us; the launch traced here: 550 us
  other arithmetic  277 us (50%)
  local copies, waits for them, and re-layouts  158 us (28%)
  waiting for transfers between devices  86.2 us (15%)
  starting transfers between devices  14.3 us (3%)
  between operations  13.9 us (2%)
    dynamic_update_slice x183, other arithmetic, thomas(): lax.scan(forward, start, (sub_diag, main_diag, super_diag, right_side))  231 us
    all_gather x2, waiting for transfers between devices, per_device(): right_all = lax.all_gather(right_part, 'gz', axis=0, tiled=True)  85.5 us
    dynamic_slice x61, local copies, waits for them, and re-layouts, thomas(): lax.scan(forward, start, (sub_diag, main_diag, super_diag, right_side))  43 us
    scatter-add x1, local copies, waits for them, and re-layouts, per_device(): source = jnp.zeros(adjoint.shape, jnp.float32).at[:, jnp.clip(local_z, 0,...  38.3 us
    broadcast_in_dim x1, local copies, waits for them, and re-layouts, per_device(): jnp.zeros(adjoint.shape, jnp.float32)  21.5 us
    scatter-add x1, other arithmetic, per_device(): source = jnp.zeros(adjoint.shape, jnp.float32).at[:, jnp.clip(local_z, 0,...  12.3 us
    ppermute x2, starting transfers between devices, padded_2(): lax.ppermute(tail, axis, [(i, (i + 1) % count) for i in range(ends)])  11.3 us
  transfers between devices with their start and end apart: 7, of which 3 were waited for; matrix products, arithmetic and copies ran while one was open for 46% of the time, Pallas kernels for 0%

commit v1 on v0

--- a/solution.py
+++ b/solution.py
@@ -6,6 +6,23 @@
 SWEEPS = 2
 PSEUDO_STEP = 0.2
 LATERAL_VISC = 1.0
+
+
+def joined_along(blocks, dim):
+    shape = list(blocks.shape[1:])
+    shape[dim] *= blocks.shape[0]
+    return jnp.moveaxis(blocks, 0, dim).reshape(shape)
+
+
+def collect(x, axis, dim):
+    size = lax.axis_size(axis)
+    right = [(i, (i + 1) % size) for i in range(size)]
+    blocks = [x]
+    while len(blocks) < size:
+        blocks.append(lax.ppermute(blocks[-1], axis, right))
+    index = lax.axis_index(axis)
+    blocks = jnp.stack(blocks)[(index - jnp.arange(size)) % size]
+    return joined_along(blocks, dim)
 
 
 def padded_2(cells, sides, width):
@@ -133,7 +150,7 @@
         right_part = jnp.concatenate(
             [local_part[0], local_part[interior - 1], stacked[z_cells - 1]], 0
         )[None]
-        right_all = lax.all_gather(right_part, "gz", axis=0, tiled=True)
+        right_all = collect(right_part, "gz", 0)
         next_first = jnp.concatenate([right_all[1:, 0:3], jnp.zeros_like(right_all[:1, 0:3])], 0)
         red_right = (
             right_all[:, 6:9]

time: 559 us -> 632 us (1.13)
  waiting for transfers between devices: 86.2 us -> 134 us
  local copies, waits for them, and re-layouts: 158 us -> 188 us
  other arithmetic: 277 us -> 268 us
    ppermute x0 -> x14, waiting for transfers between devices: none -> 133 us  [collect(): blocks.append(lax.ppermute(blocks[-1], axis, right))]
    all_gather x2 -> x0, waiting for transfers between devices: 85.5 us -> none  [per_device(): right_all = lax.all_gather(right_part, 'gz', axis=0, tiled=True)]
    unnamed x61 -> x87, local copies, waits for them, and re-layouts: 9.75 us -> 20.9 us
    gather x0 -> x2, local copies, waits for them, and re-layouts: none -> 10.1 us  [collect(): blocks = jnp.stack(blocks)[(index - jnp.arange(size)) % size]]
  transfers between devices with their start and end apart: 7 -> 19, of which waited for: 3 -> 15; matrix products, arithmetic and copies ran while one was open for 46% -> 42% of each run, Pallas kernels for 0% -> 0%
where the time goes in v1:
time: 632 us; the launch traced here: 620 us
  other arithmetic  268 us (42%)
  local copies, waits for them, and re-layouts  188 us (30%)
  waiting for transfers between devices  134 us (21%)
  starting transfers between devices  14.3 us (2%)
  between operations  14.2 us (2%)
    dynamic_update_slice x183, other arithmetic, thomas(): lax.scan(forward, start, (sub_diag, main_diag, super_diag, right_side))  230 us
    ppermute x14, waiting for transfers between devices, collect(): blocks.append(lax.ppermute(blocks[-1], axis, right))  133 us
    dynamic_slice x61, local copies, waits for them, and re-layouts, thomas(): lax.scan(forward, start, (sub_diag, main_diag, super_diag, right_side))  49 us
    scatter-add x1, local copies, waits for them, and re-layouts, per_device(): source = jnp.zeros(adjoint.shape, jnp.float32).at[:, jnp.clip(local_z, 0,...  38.3 us
    broadcast_in_dim x1, local copies, waits for them, and re-layouts, per_device(): jnp.zeros(adjoint.shape, jnp.float32)  21.4 us
    unnamed x87, local copies, waits for them, and re-layouts  20.9 us
  transfers between devices with their start and end apart: 19, of which 15 were waited for; matrix products, arithmetic and copies ran while one was open for 42% of the time, Pallas kernels for 0%

profile of v1, /device:TPU:0, one launch (start us, length us, event | category | flops | bytes accessed | tf_op | source)
XLA Modules:
  0.0 619.8 jit_solution(9735382588287443041)
XLA Ops:
  24.0 12.7 %while.174 = (s32[]{:T(128)}, f32[1,8192]{1,0:T(1,128)S(1)}, f32[2,8192]{1,0:T(2,128)S(1)}, f32[15,1,8192]{2,1,0:T(1,128)}, f32[15,2,8192]{2,1,0:T(2,128)S(1)}, ...) while((s32[]{:T(128)}, f32[1,8192]{1,0:T(1,128)S(1)}, ...), condition=%wide.region_6.7_spmd.clone, body=%wide.region_5.6_spmd.clone.sunk | while | flops 98307 | bytes 590460 | solution.py:59
  38.3 33.9 %while.175 = (s32[]{:T(128)}, f32[2,8192]{1,0:T(2,128)}, f32[15,2,8192]{2,1,0:T(2,128)S(1)}, f32[15,2,8192]{2,1,0:T(2,128)S(1)}, f32[15,1,8192]{2,1,0:T(1,128)}, /*index=5*/s32[]{:T(128)}, s32[]{:T(128)}, s32[]{:T(128)}) while((s32[]{:T(128)}, f32[2,8192]{1,0:T(2,128)}, f32[15,2,8192]{2,1,0:T(2,128)S(1)}, ...), condition=%wide.region_8.9_spmd.clone, body=%wide.region_7.8_spmd.clone.sunk | while | flops 49156 | bytes 360563 | solution.py:66
  75.5 21.4 %broadcast_in_dim.136 = f32[3,16,16,512]{0,3,2,1:T(8,128)} broadcast(f32[]{:T(128)} %constant.365.clone.1), dimensions={} | broadcast | bytes 1572868 | tf_op jit(solution)/shard_map/broadcast_in_dim | solution.py:98
  97.0 12.2 %scatter_fusion = f32[3,16,16,512]{0,3,2,1:T(8,128)} fusion(f32[3,16,16,512]{0,3,2,1:T(8,128)} %broadcast_in_dim.136, s32[100]{0:T(128)S(1)} %fusion.34, f32[100,3]{1,0:T(8,128)S(1)} %copy.71), kind=kCustom, calls=%fused_computation.2 | custom fusion | flops 300 | bytes 4800 | tf_op jit(solution)/shard_map/scatter-add | solution.py:105
  109.1 38.3 %copy.72 = f32[3,16,16,512]{3,2,1,0:T(8,128)S(1)} copy(f32[3,16,16,512]{0,3,2,1:T(8,128)} %scatter_fusion) | data formatting | bytes 3145728 | tf_op jit(solution)/shard_map/scatter-add | solution.py:105
  162.8 48.7 %while.172 = (s32[]{:T(128)}, f32[1,8192]{1,0:T(1,128)}, f32[3,8192]{1,0:T(4,128)}, f32[15,1,8192]{2,1,0:T(1,128)}, f32[15,3,8192]{2,1,0:T(4,128)S(1)}, /*index=...) while((s32[]{:T(128)}, f32[1,8192]{1,0:T(1,128)}, ...), condition=%wide.region_2.3_spmd.clone, body=%wide.region_1.2_spmd.clone.sunk | while | flops 131075 | bytes 754300 | solution.py:59
  213.2 46.2 %while.173 = (s32[]{:T(128)}, f32[3,8192]{1,0:T(4,128)}, f32[15,3,8192]{2,1,0:T(4,128)S(1)}, f32[15,3,8192]{2,1,0:T(4,128)}, f32[15,1,8192]{2,1,0:T(1,128)}, /*index=5*/s32[]{:T(128)}, s32[]{:T(128)}, s32[]{:T(128)}) while((s32[]{:T(128)}, f32[3,8192]{1,0:T(4,128)}, f32[15,3,8192]{2,1,0:T(4,128)S(1)}, f32[15,3,8192]{2,1,0:T(4,128)}, ...), condition=%wide.region_4.5_spmd.clone, body=%wide.region_3.4_spmd.clone.sunk | while | flops 73732 | bytes 524403 | solution.py:66
  271.8 9.6 %collective-permute-done.3 = f32[1,9,8192]{2,1,0:T(8,128)S(1)} collective-permute-done((f32[1,9,8192]{2,1,0:T(8,128)S(1)}, f32[1,9,8192]{2,1,0:T(8,128)S(1)}, u32[]{:S(2)}, u32[]{:S(2)}) %collective-permute-start.3) | collective-permute-done | bytes 294944 | tf_op jit(solution)/shard_map/ppermute | solution.py:22
  282.2 9.6 %collective-permute-done.4 = f32[1,9,8192]{2,1,0:T(8,128)S(1)} collective-permute-done((f32[1,9,8192]{2,1,0:T(8,128)S(1)}, f32[1,9,8192]{2,1,0:T(8,128)S(1)}, u32[]{:S(2)}, u32[]{:S(2)}) %collective-permute-start.4) | collective-permute-done | bytes 294944 | tf_op jit(solution)/shard_map/ppermute | solution.py:22
  292.6 9.6 %collective-permute-done.5 = f32[1,9,8192]{2,1,0:T(8,128)S(1)} collective-permute-done((f32[1,9,8192]{2,1,0:T(8,128)S(1)}, f32[1,9,8192]{2,1,0:T(8,128)S(1)}, u32[]{:S(2)}, u32[]{:S(2)}) %collective-permute-start.5) | collective-permute-done | bytes 294944 | tf_op jit(solution)/shard_map/ppermute | solution.py:22
  303.0 9.6 %collective-permute-done.6 = f32[1,9,8192]{2,1,0:T(8,128)S(1)} collective-permute-done((f32[1,9,8192]{2,1,0:T(8,128)S(1)}, f32[1,9,8192]{2,1,0:T(8,128)S(1)}, u32[]{:S(2)}, u32[]{:S(2)}) %collective-permute-start.6) | collective-permute-done | bytes 294944 | tf_op jit(solution)/shard_map/ppermute | solution.py:22
  313.4 9.5 %collective-permute-done.7 = f32[1,9,8192]{2,1,0:T(8,128)S(1)} collective-permute-done((f32[1,9,8192]{2,1,0:T(8,128)S(1)}, f32[1,9,8192]{2,1,0:T(8,128)S(1)}, u32[]{:S(2)}, u32[]{:S(2)}) %collective-permute-start.7) | collective-permute-done | bytes 294944 | tf_op jit(solution)/shard_map/ppermute | solution.py:22
  323.9 9.5 %collective-permute-done.8 = f32[1,9,8192]{2,1,0:T(8,128)S(1)} collective-permute-done((f32[1,9,8192]{2,1,0:T(8,128)S(1)}, f32[1,9,8192]{2,1,0:T(8,128)S(1)}, u32[]{:S(2)}, u32[]{:S(2)}) %collective-permute-start.8) | collective-permute-done | bytes 294944 | tf_op jit(solution)/shard_map/ppermute | solution.py:22
  352.1 26.2 %while.176 = (s32[]{:T(128)}, f32[1,8192]{1,0:T(1,128)}, f32[3,8192]{1,0:T(4,128)}, f32[8,1,8192]{2,1,0:T(1,128)}, f32[8,3,8192]{2,1,0:T(4,128)}, /*index=5*/f32...) while((s32[]{:T(128)}, f32[1,8192]{1,0:T(1,128)}, ...), condition=%wide.region_10.11_spmd.clone, body=%wide.region_9.10_spmd.clone.sunk | while | flops 131075 | bytes 853112 | solution.py:59
  379.5 24.9 %while.177 = (s32[]{:T(128)}, f32[3,8192]{1,0:T(4,128)}, f32[8,3,8192]{2,1,0:T(4,128)}, f32[8,3,8192]{2,1,0:T(4,128)}, f32[8,1,8192]{2,1,0:T(1,128)}, /*index=5*/s32[]{:T(128)}, s32[]{:T(128)}, s32[]{:T(128)}) while((s32[]{:T(128)}, f32[3,8192]{1,0:T(4,128)}, f32[8,3,8192]{2,1,0:T(4,128)}, f32[8,3,8192]{2,1,0:T(4,128)}, ...), condition=%wide.region_12.13_spmd.clone, body=%wide.region_11.12_spmd.clone.sunk | while | flops 73732 | bytes 622707 | solution.py:66
  428.5 29.6 %while.178 = (s32[]{:T(128)}, f32[1,8192]{1,0:T(1,128)S(1)}, f32[3,8192]{1,0:T(4,128)S(1)}, f32[15,1,8192]{2,1,0:T(1,128)S(1)}, f32[15,3,8192]{2,1,0:T(4,128)S(1...) while((s32[]{:T(128)}, f32[1,8192]{1,0:T(1,128)S(1)}, ...), condition=%wide.region_14.15_spmd.clone, body=%wide.region_13.14_spmd.clone.sunk | while | flops 131075 | bytes 819328 | solution.py:59
  459.8 16.7 %while.179 = (s32[]{:T(128)}, f32[3,8192]{1,0:T(4,128)S(1)}, f32[15,3,8192]{2,1,0:T(4,128)S(1)}, f32[15,3,8192]{2,1,0:T(4,128)}, f32[15,1,8192]{2,1,0:T(1,128)S(1)}, /*index=5*/s32[]{:T(128)}, s32[]{:T(128)}, s32[]{:T(128)}) while((s32[]{:T(128)}, f32[3,8192]{1,0:T(4,128)S(1)}, f32[15,3,8192]{2,1,0:T(4,128)S(1)}, ...), condition=%wide.region_16.17_spmd.clone, body=%wide.region_15.16_spmd.clone.sunk | while | flops 73732 | bytes 589939 | solution.py:66
  488.0 9.6 %collective-permute-done.12 = f32[1,9,8192]{2,1,0:T(8,128)S(1)} collective-permute-done((f32[1,9,8192]{2,1,0:T(8,128)S(1)}, f32[1,9,8192]{2,1,0:T(8,128)S(1)}, u32[]{:S(2)}, u32[]{:S(2)}) %collective-permute-start.12) | collective-permute-done | bytes 294944 | tf_op jit(solution)/shard_map/ppermute | solution.py:22
  498.4 9.6 %collective-permute-done.13 = f32[1,9,8192]{2,1,0:T(8,128)S(1)} collective-permute-done((f32[1,9,8192]{2,1,0:T(8,128)S(1)}, f32[1,9,8192]{2,1,0:T(8,128)S(1)}, u32[]{:S(2)}, u32[]{:S(2)}) %collective-permute-start.13) | collective-permute-done | bytes 294944 | tf_op jit(solution)/shard_map/ppermute | solution.py:22
  508.8 9.6 %collective-permute-done.14 = f32[1,9,8192]{2,1,0:T(8,128)S(1)} collective-permute-done((f32[1,9,8192]{2,1,0:T(8,128)S(1)}, f32[1,9,8192]{2,1,0:T(8,128)S(1)}, u32[]{:S(2)}, u32[]{:S(2)}) %collective-permute-start.14) | collective-permute-done | bytes 294944 | tf_op jit(solution)/shard_map/ppermute | solution.py:22
  519.2 9.6 %collective-permute-done.15 = f32[1,9,8192]{2,1,0:T(8,128)S(1)} collective-permute-done((f32[1,9,8192]{2,1,0:T(8,128)S(1)}, f32[1,9,8192]{2,1,0:T(8,128)S(1)}, u32[]{:S(2)}, u32[]{:S(2)}) %collective-permute-start.15) | collective-permute-done | bytes 294944 | tf_op jit(solution)/shard_map/ppermute | solution.py:22
  529.7 9.5 %collective-permute-done.16 = f32[1,9,8192]{2,1,0:T(8,128)S(1)} collective-permute-done((f32[1,9,8192]{2,1,0:T(8,128)S(1)}, f32[1,9,8192]{2,1,0:T(8,128)S(1)}, u32[]{:S(2)}, u32[]{:S(2)}) %collective-permute-start.16) | collective-permute-done | bytes 294944 | tf_op jit(solution)/shard_map/ppermute | solution.py:22
  563.1 20.5 %while.180 = (s32[]{:T(128)}, f32[1,8192]{1,0:T(1,128)S(1)}, f32[3,8192]{1,0:T(4,128)S(1)}, f32[8,1,8192]{2,1,0:T(1,128)}, f32[8,3,8192]{2,1,0:T(4,128)S(1)}, /*...) while((s32[]{:T(128)}, f32[1,8192]{1,0:T(1,128)S(1)}, ...), condition=%wide.region_18.19_spmd.clone, body=%wide.region_17.18_spmd.clone.sunk | while | flops 131075 | bytes 819836 | solution.py:59
  585.8 20.0 %while.181 = (s32[]{:T(128)}, f32[3,8192]{1,0:T(4,128)S(1)}, f32[8,3,8192]{2,1,0:T(4,128)}, f32[8,3,8192]{2,1,0:T(4,128)}, f32[8,1,8192]{2,1,0:T(1,128)}, /*index=5*/s32[]{:T(128)}, s32[]{:T(128)}, s32[]{:T(128)}) while((s32[]{:T(128)}, f32[3,8192]{1,0:T(4,128)S(1)}, f32[8,3,8192]{2,1,0:T(4,128)}, f32[8,3,8192]{2,1,0:T(4,128)}, ...), condition=%wide.region_20.21_spmd.clone, body=%wide.region_19.20_spmd.clone.sunk | while | flops 73732 | bytes 557171 | solution.py:66
  (457 shorter events, 427.6 us)
Async XLA Ops:
  6.5 68.7 %copy-start = (f32[3,12]{1,0:T(4,128)S(1)}, f32[3,12]{1,0:T(4,128)}, u32[]{:S(2)}) copy-start(f32[3,12]{1,0:T(4,128)} %param.37) | copy-start | bytes 436
  6.5 335.2 %all-gather.4.cloned.1.call-start = ((), (), s32[]{:S(2)}) async-start(), calls=%async_computation | async-start | bytes 2359296 | tf_op jit(solution)/shard_map/all_gather | solution.py:135
  8.8 143.4 %collective-permute-start = (f32[3,16,1,512]{3,1,2,0:T(8,128)}, f32[3,16,1,512]{3,1,2,0:T(8,128)}, u32[]{:S(2)}, u32[]{:S(2)}) collective-permute-start(f32[3,16,1,512]{3,1,2,0:T(8,128)} %copy.88), channel_id=1, source_target_pairs={{8,0},{16,8},{24,16},{9,1},{17,9},{25,17},{10,2},{18,10},{26,18},{... | collective-permute-start | bytes 294920 | tf_op jit(solution)/shard_map/ppermute | solution.py:38
  10.7 142.4 %collective-permute-start.1 = (f32[3,16,1,512]{3,1,2,0:T(8,128)}, f32[3,16,1,512]{3,1,2,0:T(8,128)}, u32[]{:S(2)}, u32[]{:S(2)}) collective-permute-start(f32[3,16,1,512]{3,1,2,0:T(8,128)} %copy.89), channel_id=1, source_target_pairs={{0,8},{8,16},{16,24},{1,9},{9,17},{17,25},{2,10},{10,18},{18,26},{... | collective-permute-start | bytes 294920 | tf_op jit(solution)/shard_map/ppermute | solution.py:36
  36.8 35.5 %copy-start.28 = (f32[1,1,16,512]{3,2,1,0:T(8,128)S(1)}, f32[1,1,16,512]{3,2,1,0:T(8,128)}, u32[]{:S(2)}) copy-start(f32[1,1,16,512]{3,2,1,0:T(8,128)} %get-tuple-element.1244) | copy-start | bytes 98308
  36.8 35.5 %copy-start.27 = (f32[1,1,16,512]{3,1,2,0:T(1,128)S(1)}, f32[1,1,16,512]{3,1,2,0:T(1,128)}, u32[]{:S(2)}) copy-start(f32[1,1,16,512]{3,1,2,0:T(1,128)} %copy-done.26) | copy-start | bytes 98308
  37.9 35.4 %copy-start.30 = (s32[3,100]{1,0:T(4,128)S(1)}, s32[3,100]{1,0:T(4,128)}, u32[]{:S(2)}) copy-start(s32[3,100]{1,0:T(4,128)} %param.35) | copy-start | bytes 3604
  260.5 10.5 %collective-permute-start.2 = (f32[1,9,8192]{2,1,0:T(8,128)S(1)}, f32[1,9,8192]{2,1,0:T(8,128)S(1)}, u32[]{:S(2)}, u32[]{:S(2)}) collective-permute-start(f32[1,9,8192]{2,1,0:T(8,128)S(1)} %fusion.22), channel_id=1, source_target_pairs={{0,1},{1,2},{2,3},{3,4},{4,5},{5,6},{6,7},{7,0},{8,9},{9,10},{10,1... | collective-permute-start | bytes 884744 | tf_op jit(solution)/shard_map/ppermute | solution.py:22
  270.9 10.4 %collective-permute-start.3 = (f32[1,9,8192]{2,1,0:T(8,128)S(1)}, f32[1,9,8192]{2,1,0:T(8,128)S(1)}, u32[]{:S(2)}, u32[]{:S(2)}) collective-permute-start(f32[1,9,8192]{2,1,0:T(8,128)S(1)} %collective-permute-done.2), channel_id=1, source_target_pairs={{0,1},{1,2},{2,3},{3,4},{4,5},{5,6},{6,7},{7,0},{8,9},{9,10},{10,1... | collective-permute-start | bytes 884744 | tf_op jit(solution)/shard_map/ppermute | solution.py:22
  281.3 10.4 %collective-permute-start.4 = (f32[1,9,8192]{2,1,0:T(8,128)S(1)}, f32[1,9,8192]{2,1,0:T(8,128)S(1)}, u32[]{:S(2)}, u32[]{:S(2)}) collective-permute-start(f32[1,9,8192]{2,1,0:T(8,128)S(1)} %collective-permute-done.3), channel_id=1, source_target_pairs={{0,1},{1,2},{2,3},{3,4},{4,5},{5,6},{6,7},{7,0},{8,9},{9,10},{10,1... | collective-permute-start | bytes 884744 | tf_op jit(solution)/shard_map/ppermute | solution.py:22
  291.7 10.4 %collective-permute-start.5 = (f32[1,9,8192]{2,1,0:T(8,128)S(1)}, f32[1,9,8192]{2,1,0:T(8,128)S(1)}, u32[]{:S(2)}, u32[]{:S(2)}) collective-permute-start(f32[1,9,8192]{2,1,0:T(8,128)S(1)} %collective-permute-done.4), channel_id=1, source_target_pairs={{0,1},{1,2},{2,3},{3,4},{4,5},{5,6},{6,7},{7,0},{8,9},{9,10},{10,1... | collective-permute-start | bytes 884744 | tf_op jit(solution)/shard_map/ppermute | solution.py:22
  302.1 10.4 %collective-permute-start.6 = (f32[1,9,8192]{2,1,0:T(8,128)S(1)}, f32[1,9,8192]{2,1,0:T(8,128)S(1)}, u32[]{:S(2)}, u32[]{:S(2)}) collective-permute-start(f32[1,9,8192]{2,1,0:T(8,128)S(1)} %collective-permute-done.5), channel_id=1, source_target_pairs={{0,1},{1,2},{2,3},{3,4},{4,5},{5,6},{6,7},{7,0},{8,9},{9,10},{10,1... | collective-permute-start | bytes 884744 | tf_op jit(solution)/shard_map/ppermute | solution.py:22
  312.5 10.4 %collective-permute-start.7 = (f32[1,9,8192]{2,1,0:T(8,128)S(1)}, f32[1,9,8192]{2,1,0:T(8,128)S(1)}, u32[]{:S(2)}, u32[]{:S(2)}) collective-permute-start(f32[1,9,8192]{2,1,0:T(8,128)S(1)} %collective-permute-done.6), channel_id=1, source_target_pairs={{0,1},{1,2},{2,3},{3,4},{4,5},{5,6},{6,7},{7,0},{8,9},{9,10},{10,1... | collective-permute-start | bytes 884744 | tf_op jit(solution)/shard_map/ppermute | solution.py:22
  322.9 10.4 %collective-permute-start.8 = (f32[1,9,8192]{2,1,0:T(8,128)S(1)}, f32[1,9,8192]{2,1,0:T(8,128)S(1)}, u32[]{:S(2)}, u32[]{:S(2)}) collective-permute-start(f32[1,9,8192]{2,1,0:T(8,128)S(1)} %collective-permute-done.7), channel_id=1, source_target_pairs={{0,1},{1,2},{2,3},{3,4},{4,5},{5,6},{6,7},{7,0},{8,9},{9,10},{10,1... | collective-permute-start | bytes 884744 | tf_op jit(solution)/shard_map/ppermute | solution.py:22
  413.0 7.5 %collective-permute-start.9 = (f32[3,16,1,512]{3,1,2,0:T(8,128)}, f32[3,16,1,512]{3,1,2,0:T(8,128)}, u32[]{:S(2)}, u32[]{:S(2)}) collective-permute-start(f32[3,16,1,512]{3,1,2,0:T(8,128)} %copy.75), channel_id=1, source_target_pairs={{8,0},{16,8},{24,16},{9,1},{17,9},{25,17},{10,2},{18,10},{26,18},{... | collective-permute-start | bytes 294920 | tf_op jit(solution)/shard_map/ppermute | solution.py:38
  414.9 7.3 %collective-permute-start.10 = (f32[3,16,1,512]{3,1,2,0:T(8,128)}, f32[3,16,1,512]{3,1,2,0:T(8,128)}, u32[]{:S(2)}, u32[]{:S(2)}) collective-permute-start(f32[3,16,1,512]{3,1,2,0:T(8,128)} %copy.77), channel_id=1, source_target_pairs={{0,8},{8,16},{16,24},{1,9},{9,17},{17,25},{2,10},{10,18},{18,26},{... | collective-permute-start | bytes 294920 | tf_op jit(solution)/shard_map/ppermute | solution.py:36
  476.7 10.5 %collective-permute-start.11 = (f32[1,9,8192]{2,1,0:T(8,128)S(1)}, f32[1,9,8192]{2,1,0:T(8,128)S(1)}, u32[]{:S(2)}, u32[]{:S(2)}) collective-permute-start(f32[1,9,8192]{2,1,0:T(8,128)S(1)} %fusion.21), channel_id=1, source_target_pairs={{0,1},{1,2},{2,3},{3,4},{4,5},{5,6},{6,7},{7,0},{8,9},{9,10},{10,1... | collective-permute-start | bytes 884744 | tf_op jit(solution)/shard_map/ppermute | solution.py:22
  487.2 10.4 %collective-permute-start.12 = (f32[1,9,8192]{2,1,0:T(8,128)S(1)}, f32[1,9,8192]{2,1,0:T(8,128)S(1)}, u32[]{:S(2)}, u32[]{:S(2)}) collective-permute-start(f32[1,9,8192]{2,1,0:T(8,128)S(1)} %collective-permute-done.11), channel_id=1, source_target_pairs={{0,1},{1,2},{2,3},{3,4},{4,5},{5,6},{6,7},{7,0},{8,9},{9,10},{10,1... | collective-permute-start | bytes 884744 | tf_op jit(solution)/shard_map/ppermute | solution.py:22
  497.6 10.4 %collective-permute-start.13 = (f32[1,9,8192]{2,1,0:T(8,128)S(1)}, f32[1,9,8192]{2,1,0:T(8,128)S(1)}, u32[]{:S(2)}, u32[]{:S(2)}) collective-permute-start(f32[1,9,8192]{2,1,0:T(8,128)S(1)} %collective-permute-done.12), channel_id=1, source_target_pairs={{0,1},{1,2},{2,3},{3,4},{4,5},{5,6},{6,7},{7,0},{8,9},{9,10},{10,1... | collective-permute-start | bytes 884744 | tf_op jit(solution)/shard_map/ppermute | solution.py:22
  508.0 10.4 %collective-permute-start.14 = (f32[1,9,8192]{2,1,0:T(8,128)S(1)}, f32[1,9,8192]{2,1,0:T(8,128)S(1)}, u32[]{:S(2)}, u32[]{:S(2)}) collective-permute-start(f32[1,9,8192]{2,1,0:T(8,128)S(1)} %collective-permute-done.13), channel_id=1, source_target_pairs={{0,1},{1,2},{2,3},{3,4},{4,5},{5,6},{6,7},{7,0},{8,9},{9,10},{10,1... | collective-permute-start | bytes 884744 | tf_op jit(solution)/shard_map/ppermute | solution.py:22
  518.4 10.4 %collective-permute-start.15 = (f32[1,9,8192]{2,1,0:T(8,128)S(1)}, f32[1,9,8192]{2,1,0:T(8,128)S(1)}, u32[]{:S(2)}, u32[]{:S(2)}) collective-permute-start(f32[1,9,8192]{2,1,0:T(8,128)S(1)} %collective-permute-done.14), channel_id=1, source_target_pairs={{0,1},{1,2},{2,3},{3,4},{4,5},{5,6},{6,7},{7,0},{8,9},{9,10},{10,1... | collective-permute-start | bytes 884744 | tf_op jit(solution)/shard_map/ppermute | solution.py:22
  528.8 10.4 %collective-permute-start.16 = (f32[1,9,8192]{2,1,0:T(8,128)S(1)}, f32[1,9,8192]{2,1,0:T(8,128)S(1)}, u32[]{:S(2)}, u32[]{:S(2)}) collective-permute-start(f32[1,9,8192]{2,1,0:T(8,128)S(1)} %collective-permute-done.15), channel_id=1, source_target_pairs={{0,1},{1,2},{2,3},{3,4},{4,5},{5,6},{6,7},{7,0},{8,9},{9,10},{10,1... | collective-permute-start | bytes 884744 | tf_op jit(solution)/shard_map/ppermute | solution.py:22
  539.2 10.4 %collective-permute-start.17 = (f32[1,9,8192]{2,1,0:T(8,128)S(1)}, f32[1,9,8192]{2,1,0:T(8,128)S(1)}, u32[]{:S(2)}, u32[]{:S(2)}) collective-permute-start(f32[1,9,8192]{2,1,0:T(8,128)S(1)} %collective-permute-done.16), channel_id=1, source_target_pairs={{0,1},{1,2},{2,3},{3,4},{4,5},{5,6},{6,7},{7,0},{8,9},{9,10},{10,1... | collective-permute-start | bytes 884744 | tf_op jit(solution)/shard_map/ppermute | solution.py:22
  585.8 21.0 %copy-start.5 = (f32[15,8192]{1,0:T(8,128)S(1)}, f32[15,8192]{1,0:T(8,128)}, u32[]{:S(2)}) copy-start(f32[15,8192]{1,0:T(8,128)} %get-tuple-element.1254) | copy-start | bytes 1474564
  (28 other events, 111.4 us)
Sparse Core Ops, SparseCore 0:
  73.4 30.1 all-gather.3
